TPU v7x, 128 devices: a whole 4x4x4 slice. The times are simulated.
128 devices in a mesh: layer: 16 (over x, y), attn: 8 (over z, core).
Axes of the slice: x: 4, y: 4, z: 4, core: 2. Of those that a mesh axis runs over, the one named last changes fastest.
Arguments:
- tokens: bfloat16 [8192, 8192], P('layer', 'attn'), may hold values from -6 to 6
- norm_gain: float32 [8192], replicated, may hold values from 0.1 to 1.9
- qkv_weight: bfloat16 [8192, 10240], P('layer', 'attn')
- doc_ids: int32 [8192], replicated, may hold values from 0 to 7, as said below
- block_server: int32 [128], replicated, may hold values from 0 to 15, as said below
Outputs:
- served: bfloat16 [8192, 8192], P('layer', 'attn')
Inputs may be any that keep to these rules, and one draw needn't show every extreme that they name: `doc_ids`: each document is a run of consecutive tokens, numbers never fall along the pack, every one of the 8 documents has at least one token, each has at most 2048 tokens and one has exactly 2048. `block_server`: the 8 stretches of one index of layer (stretches i * 8 to (i + 1) * 8 - 1) go to 8 different servers, and every server receives exactly 8 stretches. The plan is built from doc_ids to even out the causal work over servers: a stretch's cost is the number of tokens from its document's first token to its own last token, and each index of layer in turn gives its costliest stretches to the least loaded of its servers.
All inputs are finite; a program needn't handle non-finite values.
Results may differ from a plain program's by a relative error of at most 0.013.
The roundings to bfloat16 on the way count: a program that leaves them out, or rounds other values in their place, can miss the bound.
Values may be sent and summed in bfloat16 or wider, within the bound.
A program may use at most 128 MiB of HBM per device.

v0:
```python
import math

import jax
import jax.numpy as jnp
from jax import lax
from jax.sharding import PartitionSpec as P

HEAD_DIM = 128
GROUP = 8
BLOCK = 64


EPSILON = 1e-05
KEY_SPAN = 512
NEG_FLOOR = -1e30


def norm_rows(wide_rows, norm_gain):
    values_f = wide_rows.astype(jnp.float32)
    moment = jnp.mean(values_f * values_f, axis=-1, keepdims=True)
    return (values_f * lax.rsqrt(moment + EPSILON) * norm_gain).astype(jnp.bfloat16)


def attend_blocks(all_keys, all_values, doc_ids, blocks, firsts):
    count, block_len, query_cols = blocks.shape
    head_size = all_keys.shape[1]
    heads = query_cols // head_size
    total_len = all_keys.shape[0]
    key_block = math.gcd(KEY_SPAN, total_len)
    queries = blocks.reshape(count, block_len, heads, head_size).transpose(0, 2, 1, 3)
    row_first = firsts * block_len
    query_pos = row_first[:, None] + jnp.arange(block_len, dtype=jnp.int32)[None, :]
    query_doc = jnp.take(doc_ids, query_pos, axis=0)
    doc_first = jnp.sum((doc_ids[None, :] < query_doc[:, :1]).astype(jnp.int32), axis=1)
    lower = doc_first // key_block
    upper = (row_first + block_len + key_block - 1) // key_block
    spans = upper - lower
    rounds = jnp.max(spans)
    scaling = 1.0 / math.sqrt(head_size)
    offsets = jnp.arange(key_block, dtype=jnp.int32)

    def take_rows(source, first):
        return lax.dynamic_slice_in_dim(source, first, key_block, 0)

    def visit(step, running):
        run_max, sums, output = running
        active = step < spans
        key_first = jnp.minimum(lower + step, upper - 1) * key_block
        key_rows = jax.vmap(take_rows, (None, 0))(all_keys, key_first)
        value_rows = jax.vmap(take_rows, (None, 0))(all_values, key_first)
        key_doc = jax.vmap(take_rows, (None, 0))(doc_ids, key_first)
        key_pos = key_first[:, None] + offsets[None, :]
        scores = (
            jnp.einsum("bhtd,bsd->bhts", queries, key_rows, preferred_element_type=jnp.float32)
            * scaling
        )
        allowed = (
            (key_pos[:, None, :] <= query_pos[:, :, None])
            & (key_doc[:, None, :] == query_doc[:, :, None])
            & active[:, None, None]
        )
        allowed = allowed[:, None]
        masked = jnp.where(allowed, scores, NEG_FLOOR)
        new_max = jnp.maximum(run_max, jnp.max(masked, axis=-1))
        rescale = jnp.exp(run_max - new_max)
        probs = jnp.where(allowed, jnp.exp(scores - new_max[..., None]), 0.0)
        rounded = probs.astype(jnp.bfloat16)
        output = output * rescale[..., None] + jnp.einsum(
            "bhts,bsd->bhtd", rounded, value_rows, preferred_element_type=jnp.float32
        )
        sums = sums * rescale + jnp.sum(probs, axis=-1)
        return (new_max, sums, output)

    start_state = (
        jnp.full((count, heads, block_len), NEG_FLOOR, jnp.float32),
        jnp.zeros((count, heads, block_len), jnp.float32),
        jnp.zeros((count, heads, block_len, head_size), jnp.float32),
    )
    run_max, sums, output = lax.fori_loop(0, rounds, visit, start_state)
    output = output / sums[..., None]
    return output.transpose(0, 2, 1, 3).reshape(count, block_len, query_cols).astype(jnp.bfloat16)


def shards(tokens, norm_gain, qkv_weight, doc_ids, block_server):
    wide_rows = lax.all_gather(tokens, "attn", axis=1, tiled=True)
    normed = norm_rows(wide_rows, norm_gain)
    normed_cols = normed.T
    tok_rows = normed.shape[0]
    query_cols = GROUP * HEAD_DIM
    projected = lax.dot_general(
        normed_cols,
        lax.all_gather(qkv_weight, "layer", axis=0, tiled=True),
        (((0,), (0,)), ((), ())),
        preferred_element_type=jnp.float32,
    ).astype(jnp.bfloat16)
    queries = projected[:, :query_cols]
    keys_here = projected[:, query_cols : query_cols + HEAD_DIM]
    values_here = projected[:, query_cols + HEAD_DIM :]
    all_keys, all_values = (
        lax.all_gather(keys_here, "layer", axis=0, tiled=True),
        lax.all_gather(values_here, "layer", axis=0, tiled=True),
    )
    servers = lax.axis_size("layer")
    own_index = lax.axis_index("layer")
    blocks_here = tok_rows // BLOCK
    plan_table = block_server.reshape(servers, blocks_here)
    own_plan = lax.dynamic_index_in_dim(plan_table, own_index, 0, keepdims=False)
    server_ids = jnp.arange(servers, dtype=jnp.int32)
    send_pick = (own_plan[None, :] == server_ids[:, None]).astype(jnp.bfloat16)
    arriving = (plan_table == own_index).astype(jnp.int32)
    present = jnp.sum(arriving, axis=1)
    local_slot = jnp.sum(arriving * jnp.arange(blocks_here, dtype=jnp.int32)[None, :], axis=1)
    global_block = server_ids * blocks_here + local_slot
    position = jnp.cumsum(present) - 1
    keep_pick = (
        (position[None, :] == jnp.arange(blocks_here, dtype=jnp.int32)[:, None])
        & (present[None, :] == 1)
    ).astype(jnp.int32)
    served_blocks = jnp.sum(keep_pick * global_block[None, :], axis=1)
    keep_matrix = keep_pick.astype(jnp.bfloat16)
    query_blocks = queries.reshape(blocks_here, BLOCK, query_cols)
    slot_rows = lax.all_to_all(
        jnp.einsum(
            "jk,kbc->jbc", send_pick, query_blocks, preferred_element_type=jnp.float32
        ).astype(jnp.bfloat16),
        "layer",
        split_axis=0,
        concat_axis=0,
        tiled=True,
    )
    served = attend_blocks(
        all_keys,
        all_values,
        doc_ids,
        jnp.einsum(
            "rn,nbc->rbc", keep_matrix, slot_rows, preferred_element_type=jnp.float32
        ).astype(jnp.bfloat16),
        served_blocks,
    )
    return served.reshape(tok_rows, query_cols)


def solution(mesh):
    placed = (P("layer", "attn"), P(), P("layer", "attn"), P(), P())
    return jax.shard_map(
        shards, mesh=mesh, in_specs=placed, out_specs=P("layer", "attn"), check_vma=False
    )
```

profile of v0, /device:TPU:2, one launch (start us, length us, event | category | flops | bytes accessed | tf_op | source)
XLA Modules:
  0.0 618.6 jit_solution(14864155308707125176)
XLA Ops:
  8.1 53.3 %all-gather.5.cloned.1.call-done = bf16[512,8192]{1,0:T(8,128)(2,1)} async-done(((bf16[512,1024]{1,0:T(8,128)(2,1)}), bf16[512,8192]{1,0:T(8,128)(2,1)}) %all-gather.5.cloned.1.call-update) | async-done | bytes 8388624 | tf_op jit(solution)/shard_map/all_gather | solution.py:85
  61.3 5.1 fusion.22
  66.5 129.8 %all-gather.7.cloned.1.call-done = bf16[8192,1280]{1,0:T(8,128)(2,1)} async-done(((bf16[512,1280]{1,0:T(8,128)(2,1)}), bf16[8192,1280]{1,0:T(8,128)(2,1)}) %all-gather.7.cloned.1.call-update) | async-done | bytes 20971536 | tf_op jit(solution)/shard_map/all_gather | solution.py:92
  196.2 16.7 %fusion.29 = bf16[512,1280]{1,0:T(8,128)(2,1)S(1)} fusion(bf16[8192,1280]{1,0:T(8,128)(2,1)} %all-gather.7.cloned.1.call-done, bf16[512,8192]{1,0:T(8,128)(2,1)} %all-gather.5.cloned.1.call-done, f32[8192]{0:T(1024)S(1)} %copy-done.4, f32[512]{0:T(512)S(1)} %add_rsqrt_fusion), kind=kOutput, calls=%fused_computation.42 | convolution fusion | flops 10754850816 | bytes 30705664 | tf_op jit(solution)/shard_map/dot_general | solution.py:90
  215.4 2.5 copy.20
  217.9 5.8 all-to-all-start
  224.3 3.1 gather_fusion
  228.6 25.0 %all-to-all-done = bf16[16,64,1024]{2,1,0:T(8,128)(2,1)S(1)} async-done(((bf16[16,64,1024]{2,1,0:T(8,128)(2,1)}), bf16[16,64,1024]{2,1,0:T(8,128)(2,1)S(1)}, u32[]{:S(2)}, u32[]{:S(2)}) %all-to-all-start) | async-done | bytes 2097184 | tf_op jit(solution)/shard_map/all_to_all | solution.py:122
  255.5 20.7 %all-gather.11.cloned.1.call-done = bf16[8192,128]{1,0:T(8,128)(2,1)} async-done(((bf16[512,128]{1,0:T(8,128)(2,1)}), bf16[8192,128]{1,0:T(8,128)(2,1)}) %all-gather.11.cloned.1.call-update) | async-done | bytes 2097168 | tf_op jit(solution)/shard_map/all_gather | solution.py:101
  276.3 46.2 %all-gather.9.cloned.1.call-done = bf16[8192,128]{1,0:T(8,128)(2,1)} async-done(((bf16[512,128]{1,0:T(8,128)(2,1)}), bf16[8192,128]{1,0:T(8,128)(2,1)}) %all-gather.9.cloned.1.call-update) | async-done | bytes 2097168 | tf_op jit(solution)/shard_map/all_gather | solution.py:100
  324.1 284.0 %while.29 = (s32[]{:T(128)}, f32[8,8,64]{2,1,0:T(8,128)S(1)}, f32[8,8,64]{2,1,0:T(8,128)S(1)}, f32[8,8,64,128]{3,2,1,0:T(8,128)}, s32[]{:T(128)}, /*index=5*/s32...) while((s32[]{:T(128)}, f32[8,8,64]{2,1,0:T(8,128)S(1)}, ...), condition=%wide.region_10.11_spmd.clone, body=%wide.region_7.10_spmd.clone.sunk | while | flops 1098920448 | bytes 53279792 | solution.py:79
  325.0 11.3 %while.30 = (s32[]{:T(128)}, s32[8192]{0:T(1024)S(1)}, s32[8,1]{0,1:T(1,128)S(1)}, s32[8,512]{1,0:T(8,128)S(1)}, s32[]{:T(128)}, /*index=5*/s32[]{:T(128)}) while((s32[]{:T(128)}, s32[8192]{0:T(1024)S(1)}, s32[8,1]{0,1:T(1,128)S(1)}, s32[8,512]{1,0:T(8,128)S(1)}, s32[]{:T(128)}, /*index=5*/s32[]{:T(128)}) %tuple.91), condition=%wide.while_cond, body=%wide.while_body.sunk | while | flops 2 | bytes 8289 | solution.py:43
  336.8 17.7 %while.31 = (s32[]{:T(128)}, bf16[8192,128]{1,0:T(8,128)(2,1)}, s32[8,2]{0,1:T(2,128)S(1)}, bf16[8,512,128]{2,1,0:T(8,128)(2,1)S(1)}, s32[]{:T(128)}) while((s32[]{:T(128)}, bf16[8192,128]{1,0:T(8,128)(2,1)}, s32[8,2]{0,1:T(2,128)S(1)}, bf16[8,512,128]{2,1,0:T(8,128)(2,1)S(1)}, s32[]{:T(128)}) %tuple.94), condition=%wide.while_cond.1, body=%wide.while_body.1.sunk | while | flops 2 | bytes 262249 | solution.py:43
  337.4 1.6 bitcast_dynamic-update-slice_fusion.4
  344.0 1.6 bitcast_dynamic-update-slice_fusion.4
  348.5 1.6 bitcast_dynamic-update-slice_fusion.4
  352.9 1.6 bitcast_dynamic-update-slice_fusion.4
  354.6 17.7 %while.32 = (s32[]{:T(128)}, bf16[8192,128]{1,0:T(8,128)(2,1)}, s32[8,2]{0,1:T(2,128)S(1)}, bf16[8,512,128]{2,1,0:T(8,128)(2,1)S(1)}, s32[]{:T(128)}) while((s32[]{:T(128)}, bf16[8192,128]{1,0:T(8,128)(2,1)}, s32[8,2]{0,1:T(2,128)S(1)}, bf16[8,512,128]{2,1,0:T(8,128)(2,1)S(1)}, s32[]{:T(128)}) %tuple.115), condition=%wide.while_cond.2, body=%wide.while_body.2.sunk | while | flops 2 | bytes 262249 | solution.py:43
  364.1 1.6 bitcast_dynamic-update-slice_fusion.5
  368.5 1.6 bitcast_dynamic-update-slice_fusion.5
  373.8 2.5 fusion.67
  376.4 3.1 multiply_add_fusion.6
  381.7 11.3 %while.30 = (s32[]{:T(128)}, s32[8192]{0:T(1024)S(1)}, s32[8,1]{0,1:T(1,128)S(1)}, s32[8,512]{1,0:T(8,128)S(1)}, s32[]{:T(128)}, /*index=5*/s32[]{:T(128)}) while((s32[]{:T(128)}, s32[8192]{0:T(1024)S(1)}, s32[8,1]{0,1:T(1,128)S(1)}, s32[8,512]{1,0:T(8,128)S(1)}, s32[]{:T(128)}, /*index=5*/s32[]{:T(128)}) %tuple.91), condition=%wide.while_cond, body=%wide.while_body.sunk | while | flops 2 | bytes 8289 | solution.py:43
  393.4 17.7 %while.31 = (s32[]{:T(128)}, bf16[8192,128]{1,0:T(8,128)(2,1)}, s32[8,2]{0,1:T(2,128)S(1)}, bf16[8,512,128]{2,1,0:T(8,128)(2,1)S(1)}, s32[]{:T(128)}) while((s32[]{:T(128)}, bf16[8192,128]{1,0:T(8,128)(2,1)}, s32[8,2]{0,1:T(2,128)S(1)}, bf16[8,512,128]{2,1,0:T(8,128)(2,1)S(1)}, s32[]{:T(128)}) %tuple.94), condition=%wide.while_cond.1, body=%wide.while_body.1.sunk | while | flops 2 | bytes 262249 | solution.py:43
  394.0 1.6 bitcast_dynamic-update-slice_fusion.4
  398.5 1.6 bitcast_dynamic-update-slice_fusion.4
  402.9 1.6 bitcast_dynamic-update-slice_fusion.4
  407.3 1.6 bitcast_dynamic-update-slice_fusion.4
  411.3 17.7 %while.32 = (s32[]{:T(128)}, bf16[8192,128]{1,0:T(8,128)(2,1)}, s32[8,2]{0,1:T(2,128)S(1)}, bf16[8,512,128]{2,1,0:T(8,128)(2,1)S(1)}, s32[]{:T(128)}) while((s32[]{:T(128)}, bf16[8192,128]{1,0:T(8,128)(2,1)}, s32[8,2]{0,1:T(2,128)S(1)}, bf16[8,512,128]{2,1,0:T(8,128)(2,1)S(1)}, s32[]{:T(128)}) %tuple.115), condition=%wide.while_cond.2, body=%wide.while_body.2.sunk | while | flops 2 | bytes 262249 | solution.py:43
  414.1 1.6 bitcast_dynamic-update-slice_fusion.5
  418.6 1.6 bitcast_dynamic-update-slice_fusion.5
  423.0 1.6 bitcast_dynamic-update-slice_fusion.5
  427.4 1.6 bitcast_dynamic-update-slice_fusion.5
  430.5 2.5 fusion.67
  433.1 3.1 multiply_add_fusion.6
  438.3 11.3 %while.30 = (s32[]{:T(128)}, s32[8192]{0:T(1024)S(1)}, s32[8,1]{0,1:T(1,128)S(1)}, s32[8,512]{1,0:T(8,128)S(1)}, s32[]{:T(128)}, /*index=5*/s32[]{:T(128)}) while((s32[]{:T(128)}, s32[8192]{0:T(1024)S(1)}, s32[8,1]{0,1:T(1,128)S(1)}, s32[8,512]{1,0:T(8,128)S(1)}, s32[]{:T(128)}, /*index=5*/s32[]{:T(128)}) %tuple.91), condition=%wide.while_cond, body=%wide.while_body.sunk | while | flops 2 | bytes 8289 | solution.py:43
  450.1 17.7 %while.31 = (s32[]{:T(128)}, bf16[8192,128]{1,0:T(8,128)(2,1)}, s32[8,2]{0,1:T(2,128)S(1)}, bf16[8,512,128]{2,1,0:T(8,128)(2,1)S(1)}, s32[]{:T(128)}) while((s32[]{:T(128)}, bf16[8192,128]{1,0:T(8,128)(2,1)}, s32[8,2]{0,1:T(2,128)S(1)}, bf16[8,512,128]{2,1,0:T(8,128)(2,1)S(1)}, s32[]{:T(128)}) %tuple.94), condition=%wide.while_cond.1, body=%wide.while_body.1.sunk | while | flops 2 | bytes 262249 | solution.py:43
  450.7 1.6 bitcast_dynamic-update-slice_fusion.4
  455.1 1.6 bitcast_dynamic-update-slice_fusion.4
  468.0 17.7 %while.32 = (s32[]{:T(128)}, bf16[8192,128]{1,0:T(8,128)(2,1)}, s32[8,2]{0,1:T(2,128)S(1)}, bf16[8,512,128]{2,1,0:T(8,128)(2,1)S(1)}, s32[]{:T(128)}) while((s32[]{:T(128)}, bf16[8192,128]{1,0:T(8,128)(2,1)}, s32[8,2]{0,1:T(2,128)S(1)}, bf16[8,512,128]{2,1,0:T(8,128)(2,1)S(1)}, s32[]{:T(128)}) %tuple.115), condition=%wide.while_cond.2, body=%wide.while_body.2.sunk | while | flops 2 | bytes 262249 | solution.py:43
  470.8 1.6 bitcast_dynamic-update-slice_fusion.5
  475.2 1.6 bitcast_dynamic-update-slice_fusion.5
  487.2 2.5 fusion.67
  489.8 3.1 multiply_add_fusion.6
  495.0 11.3 %while.30 = (s32[]{:T(128)}, s32[8192]{0:T(1024)S(1)}, s32[8,1]{0,1:T(1,128)S(1)}, s32[8,512]{1,0:T(8,128)S(1)}, s32[]{:T(128)}, /*index=5*/s32[]{:T(128)}) while((s32[]{:T(128)}, s32[8192]{0:T(1024)S(1)}, s32[8,1]{0,1:T(1,128)S(1)}, s32[8,512]{1,0:T(8,128)S(1)}, s32[]{:T(128)}, /*index=5*/s32[]{:T(128)}) %tuple.91), condition=%wide.while_cond, body=%wide.while_body.sunk | while | flops 2 | bytes 8289 | solution.py:43
  506.8 17.7 %while.31 = (s32[]{:T(128)}, bf16[8192,128]{1,0:T(8,128)(2,1)}, s32[8,2]{0,1:T(2,128)S(1)}, bf16[8,512,128]{2,1,0:T(8,128)(2,1)S(1)}, s32[]{:T(128)}) while((s32[]{:T(128)}, bf16[8192,128]{1,0:T(8,128)(2,1)}, s32[8,2]{0,1:T(2,128)S(1)}, bf16[8,512,128]{2,1,0:T(8,128)(2,1)S(1)}, s32[]{:T(128)}) %tuple.94), condition=%wide.while_cond.1, body=%wide.while_body.1.sunk | while | flops 2 | bytes 262249 | solution.py:43
  507.4 1.6 bitcast_dynamic-update-slice_fusion.4
  511.8 1.6 bitcast_dynamic-update-slice_fusion.4
  524.6 17.7 %while.32 = (s32[]{:T(128)}, bf16[8192,128]{1,0:T(8,128)(2,1)}, s32[8,2]{0,1:T(2,128)S(1)}, bf16[8,512,128]{2,1,0:T(8,128)(2,1)S(1)}, s32[]{:T(128)}) while((s32[]{:T(128)}, bf16[8192,128]{1,0:T(8,128)(2,1)}, s32[8,2]{0,1:T(2,128)S(1)}, bf16[8,512,128]{2,1,0:T(8,128)(2,1)S(1)}, s32[]{:T(128)}) %tuple.115), condition=%wide.while_cond.2, body=%wide.while_body.2.sunk | while | flops 2 | bytes 262249 | solution.py:43
  527.4 1.6 bitcast_dynamic-update-slice_fusion.5
  531.9 1.6 bitcast_dynamic-update-slice_fusion.5
  543.8 2.5 fusion.67
  546.4 3.1 multiply_add_fusion.6
  551.7 11.3 %while.30 = (s32[]{:T(128)}, s32[8192]{0:T(1024)S(1)}, s32[8,1]{0,1:T(1,128)S(1)}, s32[8,512]{1,0:T(8,128)S(1)}, s32[]{:T(128)}, /*index=5*/s32[]{:T(128)}) while((s32[]{:T(128)}, s32[8192]{0:T(1024)S(1)}, s32[8,1]{0,1:T(1,128)S(1)}, s32[8,512]{1,0:T(8,128)S(1)}, s32[]{:T(128)}, /*index=5*/s32[]{:T(128)}) %tuple.91), condition=%wide.while_cond, body=%wide.while_body.sunk | while | flops 2 | bytes 8289 | solution.py:43
  563.4 17.7 %while.31 = (s32[]{:T(128)}, bf16[8192,128]{1,0:T(8,128)(2,1)}, s32[8,2]{0,1:T(2,128)S(1)}, bf16[8,512,128]{2,1,0:T(8,128)(2,1)S(1)}, s32[]{:T(128)}) while((s32[]{:T(128)}, bf16[8192,128]{1,0:T(8,128)(2,1)}, s32[8,2]{0,1:T(2,128)S(1)}, bf16[8,512,128]{2,1,0:T(8,128)(2,1)S(1)}, s32[]{:T(128)}) %tuple.94), condition=%wide.while_cond.1, body=%wide.while_body.1.sunk | while | flops 2 | bytes 262249 | solution.py:43
  570.7 1.6 bitcast_dynamic-update-slice_fusion.4
  575.1 1.6 bitcast_dynamic-update-slice_fusion.4
  579.5 1.6 bitcast_dynamic-update-slice_fusion.4
  581.3 17.7 %while.32 = (s32[]{:T(128)}, bf16[8192,128]{1,0:T(8,128)(2,1)}, s32[8,2]{0,1:T(2,128)S(1)}, bf16[8,512,128]{2,1,0:T(8,128)(2,1)S(1)}, s32[]{:T(128)}) while((s32[]{:T(128)}, bf16[8192,128]{1,0:T(8,128)(2,1)}, s32[8,2]{0,1:T(2,128)S(1)}, bf16[8,512,128]{2,1,0:T(8,128)(2,1)S(1)}, s32[]{:T(128)}) %tuple.115), condition=%wide.while_cond.2, body=%wide.while_body.2.sunk | while | flops 2 | bytes 262249 | solution.py:43
  590.8 1.6 bitcast_dynamic-update-slice_fusion.5
  595.2 1.6 bitcast_dynamic-update-slice_fusion.5
  600.5 2.5 fusion.67
  603.1 3.1 multiply_add_fusion.6
  608.1 2.0 fusion.41
  (461 shorter events, 217.0 us)
Async XLA Ops:
  6.5 189.7 %copy-start.4 = (f32[8192]{0:T(1024)S(1)}, f32[8192]{0:T(1024)}, u32[]{:S(2)}) copy-start(f32[8192]{0:T(1024)} %param.8) | copy-start | bytes 98308
  6.5 54.8 %all-gather.5.cloned.1.call-start = ((), (), s32[]{:S(2)}) async-start(), calls=%async_computation.1 | async-start | bytes 9437184 | tf_op jit(solution)/shard_map/all_gather | solution.py:85
  7.3 189.0 %all-gather.7.cloned.1.call-start = ((), (), s32[]{:S(2)}) async-start(), calls=%async_computation.2 | async-start | bytes 22282240 | tf_op jit(solution)/shard_map/all_gather | solution.py:92
  8.0 268.3 %all-gather.11.cloned.1.call-start = ((), (), s32[]{:S(2)}) async-start(), calls=%async_computation.4 | async-start | bytes 2228224 | tf_op jit(solution)/shard_map/all_gather | solution.py:101
  66.5 147.8 %copy-start.3 = (s32[128]{0:T(128)S(1)}, s32[128]{0:T(128)}, u32[]{:S(2)}) copy-start(s32[128]{0:T(128)} %param.11) | copy-start | bytes 1540
  212.9 11.4 %copy-start = (s32[8192]{0:T(1024)S(1)}, s32[8192]{0:T(1024)}, u32[]{:S(2)}) copy-start(s32[8192]{0:T(1024)} %param.10) | copy-start | bytes 98308
  213.6 108.8 %all-gather.9.cloned.1.call-start = ((), (), s32[]{:S(2)}) async-start(), calls=%async_computation.3 | async-start | bytes 2228224 | tf_op jit(solution)/shard_map/all_gather | solution.py:100
  217.9 35.7 %all-to-all-start = ((bf16[16,64,1024]{2,1,0:T(8,128)(2,1)}), bf16[16,64,1024]{2,1,0:T(8,128)(2,1)S(1)}, u32[]{:S(2)}, u32[]{:S(2)}) async-start(bf16[16,64,1024]{2,1,0:T(8,128)(2,1)} %copy.20), calls=%async_computation | async-start | bytes 4194304 | tf_op jit(solution)/shard_map/all_to_all | solution.py:122
  372.4 4.1 copy-start.1
  379.6 1.3 copy-start.2
  429.0 4.1 copy-start.1
  436.2 1.3 copy-start.2
  485.7 4.1 copy-start.1
  492.9 1.3 copy-start.2
  542.4 4.1 copy-start.1
  549.6 1.3 copy-start.2
  599.0 4.1 copy-start.1
  606.2 1.3 copy-start.2
Sparse Core Ops, SparseCore 0:
  9.1 52.2 all-gather.4
  63.5 132.6 all-gather.6
  213.8 62.4 all-gather.10
  278.3 44.1 all-gather.8
where the time goes:
time: 621 us; the launch traced here: 619 us
  waiting for transfers between devices  277 us (45%)
  local copies, waits for them, and re-layouts  251 us (40%)
  matrix products  41.8 us (7%)
  other arithmetic  23.8 us (4%)
  between operations  13.2 us (2%)
  loops' own time  6.3 us (1%)
    gather x360, local copies, waits for them, and re-layouts  231 us
    all_gather x1, waiting for transfers between devices, shards(): lax.all_gather(qkv_weight, 'layer', axis=0, tiled=True)  130 us
    all_gather x1, waiting for transfers between devices, shards(): wide_rows = lax.all_gather(tokens, 'attn', axis=1, tiled=True)  53.3 us
    all_gather x1, waiting for transfers between devices, shards(): lax.all_gather(keys_here, 'layer', axis=0, tiled=True)  46.2 us
    all_to_all x1, waiting for transfers between devices, shards(): lax.all_to_all(jnp.einsum('jk,kbc->jbc', send_pick, query_blocks, preferr...  25 us
    all_gather x1, waiting for transfers between devices, shards(): lax.all_gather(values_here, 'layer', axis=0, tiled=True)  20.7 us
    dot_general x1, matrix products, shards(): lax.dot_general(normed_cols, lax.all_gather(qkv_weight, 'layer', axis=0,...  16.7 us
    dot_general x5, matrix products, visit(): jnp.einsum('bhts,bsd->bhtd', rounded, value_rows, preferred_element_type=...  15.7 us
  transfers between devices with their start and end apart: 5, of which 5 were waited for; matrix products, arithmetic and copies ran while one was open for 3% of the time, Pallas kernels for 0%

commit v1 on v0

v1 whole, which is shorter than its diff:
```python
import math

import jax
import jax.numpy as jnp
from jax import lax
from jax.experimental import pallas as pl
from jax.experimental.pallas import tpu as pltpu
from jax.sharding import PartitionSpec as P

MESH = pl.DeviceIdType.MESH
HEAD_DIM = 128
GROUP = 8
BLOCK = 64
STEP = 512
BACK = 4
RING = 4
LAYERS = 16
ATTN = 8
ROWS = 512
COLS = 1024
WIDE = 256
CHUNKS = 5
HALF = 256

EPSILON = 1e-05
LOG2E = math.log2(math.e)
NEG_FLOOR = -1e30 * LOG2E
MASKED = -3e38
SCALING = LOG2E / math.sqrt(HEAD_DIM)


def remote(src, dst, send_sem, recv_sem, **device):
    return pltpu.make_async_remote_copy(
        src_ref=src,
        dst_ref=dst,
        send_sem=send_sem,
        recv_sem=recv_sem,
        device_id=device,
        device_id_type=MESH,
    )


def fused_kernel(
    tok_ref,
    gain_ref,
    w_ref,
    doc_ref,
    plan_ref,
    out_ref,
    mine,
    normed,
    weights,
    keys,
    values,
    bias,
    pick,
    keep,
    attended,
    slots,
    landed,
    acc,
    moments,
    own_sem,
    pair_send,
    pair_recv,
    w_send,
    w_recv,
    core_send,
    core_recv,
    share_send,
    share_recv,
    t_send,
    t_recv,
    m_send,
    m_recv,
    kv_send,
    kv_recv,
    s_send,
    s_recv,
):
    layer = lax.axis_index("layer")
    attn = lax.axis_index("attn")
    x, y = layer // RING, layer % RING
    z, core = attn // 2, attn % 2
    side = y // 2
    partner = x * RING + 3 - y
    inner = x * RING + y + 1 - 2 * (y % 2)
    unit = ((y + 1) // 2) % 2
    same = 1 - (core - side) * (core - side)
    home, away = core == side, core != side
    rows_at = same * layer + (1 - same) * partner
    sibling = attn + 1 - 2 * core
    group = 2 * z + side

    def holder(row):
        row = row % LAYERS
        across, along = row // RING, row % RING
        inside = 1 - (along // 2 - side) * (along // 2 - side)
        along = inside * along + (1 - inside) * (3 - along)
        core_there = inside * side + (1 - inside) * (1 - side)
        return {"layer": across * RING + along, "attn": 2 * z + core_there}

    def across_x(step):
        return {"layer": ((x + step) % RING) * RING + y}

    def along_z(step):
        return {"attn": (attn + 2 * step) % ATTN}

    shift = (1, -1)
    sent = {"all": [], "home": [], "away": [], 0: [], 1: []}
    condition = {"home": home, "away": away, 0: core == 0, 1: core == 1}

    def go(copies, who="all"):
        if who == "all":
            for copy in copies:
                copy.start()
        else:

            @pl.when(condition[who])
            def _():
                for copy in copies:
                    copy.start()

        sent[who].extend(copies)

    def arrive(copies, who="all"):
        if who == "all":
            for copy in copies:
                copy.wait_recv()
        else:

            @pl.when(condition[who])
            def _():
                for copy in copies:
                    copy.wait_recv()

    barrier = pltpu.get_barrier_semaphore()
    for step in range(1, LAYERS):
        for at in (attn, sibling):
            pl.semaphore_signal(
                barrier,
                inc=1,
                device_id={"layer": (layer + step) % LAYERS, "attn": at},
                device_id_type=MESH,
            )
    for step in range(1, ATTN):
        pl.semaphore_signal(
            barrier, inc=1, device_id={"attn": (attn + step) % ATTN}, device_id_type=MESH
        )
    pl.semaphore_wait(barrier, 2 * (LAYERS - 1) + ATTN - 1)

    def columns(chunk):
        first = GROUP * HEAD_DIM if chunk == 0 else (chunk - 1) * WIDE
        return pl.ds(first, WIDE)

    def w_pair(chunk):
        def share(half):
            rows = pl.ds(pl.multiple_of(half * HALF, HALF), HALF)
            return w_ref.at[rows, columns(chunk)], weights.at[chunk, half, x, unit, side]

        src, dst = share(1 - core)
        go(
            [
                remote(
                    src,
                    dst,
                    pair_send.at[chunk, 0],
                    pair_recv.at[chunk, 1 - same],
                    layer=rows_at,
                    attn=sibling,
                )
            ]
        )
        src, dst = share(core)
        go(
            [
                remote(
                    src,
                    dst,
                    pair_send.at[chunk, 1],
                    pair_recv.at[chunk, 1],
                    layer=partner,
                    attn=attn,
                )
            ],
            "away",
        )
        own = pltpu.make_async_copy(src, dst, own_sem.at[chunk])

        @pl.when(home)
        def _():
            own.start()

        return own

    def w_legs(chunk):
        ring = [across_x(shift[way]) for way in range(2)]
        cols = [x, (x - 1) % RING, (x + 1) % RING, (x + 2) % RING]

        def leg(ref, index, device):
            return remote(
                ref, ref, w_send.at[chunk, index], w_recv.at[chunk, index], **device
            )

        inside = {"layer": inner}
        first = {0: {}, 1: {}}
        units = [weights.at[chunk, 0, cols[k], unit] for k in range(4)]
        first[0]["near"] = [leg(units[0], way, ring[way]) for way in range(2)]
        first[0]["far"] = [
            leg(weights.at[chunk, 0, cols[1 + way], unit, way], 3 + way, ring[way])
            for way in range(2)
        ]
        first[0]["inner"] = [leg(units[k], (2, 5, 6, 7)[k], inside) for k in range(4)]
        first[1]["inner"] = [leg(weights.at[chunk, 1, x, unit], 0, inside)]
        first[1]["near"] = [leg(weights.at[chunk, 1, x], 1 + way, ring[way]) for way in range(2)]
        first[1]["far"] = [
            leg(weights.at[chunk, 1, cols[1 + way], way], 3 + way, ring[way]) for way in range(2)
        ]
        first["core"] = [
            remote(
                weights.at[chunk, core, cols[k]],
                weights.at[chunk, core, cols[k]],
                core_send.at[chunk, k],
                core_recv.at[chunk, k],
                attn=sibling,
            )
            for k in range(4)
        ]
        return first

    own_copies = {}
    legs = {}

    def w_start(chunk):
        own_copies[chunk] = w_pair(chunk)

    def w_one(chunk):
        legs[chunk] = w_legs(chunk)
        got = legs[chunk]
        place = weights.at[chunk, core, x, unit, side]
        from_core = remote(
            place, place, pair_send.at[chunk, 0], pair_recv.at[chunk, 0], attn=sibling
        )
        from_pair = remote(
            place, place, pair_send.at[chunk, 0], pair_recv.at[chunk, 1], layer=partner
        )

        @pl.when(home)
        def _():
            own_copies[chunk].wait()

        arrive([from_core], "away")
        arrive([from_pair])
        go([got[0]["near"][0], got[0]["near"][1], got[0]["inner"][0]], 0)
        go(got[1]["inner"], 1)

    def w_two(chunk):
        got = legs[chunk]
        for way in range(2):
            arrive([got[0]["near"][way]], 0)
            go([got[0]["far"][way], got[0]["inner"][1 + way]], 0)
        arrive(got[1]["inner"], 1)
        go(got[1]["near"] + [], 1)
        go([got["core"][0]], 1)

    def w_three(chunk):
        got = legs[chunk]
        arrive(got[0]["far"], 0)
        go([got[0]["inner"][3]], 0)
        for k in range(3):
            arrive([got[0]["inner"][k]], 0)
            go([got["core"][k]], 0)
        for way in range(2):
            arrive([got[1]["near"][way]], 1)
            go([got[1]["far"][way], got["core"][1 + way]], 1)

    def w_four(chunk):
        got = legs[chunk]
        arrive([got[0]["inner"][3]], 0)
        arrive(got[1]["far"], 1)
        go([got["core"][3]])

    def w_wait(chunk):
        arrive(legs[chunk]["core"])

    w_start(0)
    w_start(1)

    tokens = tok_ref[...].astype(jnp.float32)
    own_sum = jnp.sum(tokens * tokens, axis=1, keepdims=True)
    moments[attn] = jnp.transpose(jnp.broadcast_to(own_sum, (ROWS, 128)))[:8]
    m_copies = [
        remote(
            moments.at[attn],
            moments.at[attn],
            m_send.at[step - 1],
            m_recv.at[step - 1],
            attn=(attn + step) % ATTN,
        )
        for step in range(1, ATTN)
    ]
    go(m_copies)
    acc[...] = jnp.zeros_like(acc)
    arrive(m_copies)
    total = moments[0]
    for at in range(1, ATTN):
        total = total + moments[at]
    total = jnp.transpose(jnp.broadcast_to(total[:1], (128, ROWS)))[:, :1]
    scale = lax.rsqrt(total * (1.0 / (ATTN * COLS)) + EPSILON)
    gain = gain_ref[pl.ds(pl.multiple_of(attn * COLS, COLS), COLS)].reshape(1, COLS)
    mine[...] = (tok_ref[...].astype(jnp.float32) * scale * gain).astype(jnp.bfloat16)

    def share_copy(half, index, **device):
        rows = pl.ds(half * HALF, HALF)
        return remote(
            mine.at[rows],
            normed.at[attn, rows],
            share_send.at[index, half],
            share_recv.at[core, half],
            **device,
        )

    for half in range(2):
        go([share_copy(half, 0, layer=partner, attn=group)])
        go([share_copy(half, 1, attn=sibling)], "away")

    @pl.when(home)
    def _():
        normed[attn] = mine[...]

    def share_wait(which, half):
        rows = normed.at[2 * z + which, pl.ds(half * HALF, HALF)]
        return remote(
            rows, rows, share_send.at[0, half], share_recv.at[which, half], layer=partner
        )

    def z_rows(block, half):
        return normed.at[pl.ds(2 * (block % RING), 2), pl.ds(half * HALF, HALF)]

    def z_copy(ref, index, way):
        return remote(ref, ref, t_send.at[index], t_recv.at[index], **along_z(shift[way]))

    z_near = {
        (half, way): z_copy(z_rows(z, half), 2 * half + way, way)
        for half in range(2)
        for way in range(2)
    }
    z_far = [z_copy(z_rows(z - shift[way], way), 4 + way, way) for way in range(2)]
    share_pair = {half: [share_wait(0, half), share_wait(1, half)] for half in range(2)}
    share_core = {half: [share_wait(1 - core, half)] for half in range(2)}

    def z_start(who, half):
        arrive(share_core[half] if who == "home" else share_pair[half], who)
        go([z_near[half, 0], z_near[half, 1]], who)

    def z_forward(who, way):
        arrive([z_near[way, way]], who)
        go([z_far[way]], who)

    z_start("home", 0)
    z_start("home", 1)
    w_start(2)
    w_one(0)
    w_two(0)
    w_one(1)

    def one_hot(table, first, second, at):
        rows = table.shape[0]
        row_at = lax.broadcasted_iota(jnp.int32, (rows, 128), 0)
        col_at = lax.broadcasted_iota(jnp.int32, (rows, 128), 1)
        wanted = jnp.where(col_at < BLOCK, first, second)
        hit = (row_at // BLOCK == wanted) & (row_at % BLOCK == col_at % BLOCK)
        table[:, at * 128 : (at + 1) * 128] = jnp.where(hit, 1.0, 0.0).astype(jnp.bfloat16)

    blocks = ROWS // BLOCK
    for at in range(blocks // 2):
        first = rows_at * blocks + 2 * at
        one_hot(pick, plan_ref[first], plan_ref[first + 1], at)

    z_start("away", 0)
    w_three(0)
    w_two(1)

    places = []
    count = 0
    for source in range(LAYERS):
        present = 0
        for at in range(blocks):
            present = present + jnp.where(plan_ref[source * blocks + at] == layer, 1, 0)
        places.append(jnp.where(present == 1, count, -1))
        count = count + present
    for at in range(LAYERS // 2):
        one_hot(keep, places[2 * at], places[2 * at + 1], at)

    def doc_row(source):
        row = doc_ref[pl.ds(pl.multiple_of(source * STEP, STEP), STEP)]
        return row.reshape(1, STEP).astype(jnp.float32)

    row_doc = jnp.transpose(jnp.broadcast_to(doc_row(rows_at), (128, STEP)))[:, :1]
    row_at = lax.broadcasted_iota(jnp.int32, (ROWS, STEP), 0)
    key_at = lax.broadcasted_iota(jnp.int32, (ROWS, STEP), 1)
    for j in range(BACK + 1):
        source = rows_at - BACK + j
        key_doc = doc_row((source + LAYERS) % LAYERS)
        allowed = jnp.where(source < 0, -1.0, key_doc) == row_doc
        if j == BACK:
            allowed = allowed & (key_at <= row_at)
        bias[j] = jnp.where(allowed, 0.0, MASKED)

    def project(chunks, first, count):
        low, many = chunks

        @pl.loop(0, 2 * count * many)
        def _(at):
            place = at % 2
            block = (z + first + 2 * ((at // 2) % count)) % RING
            chunk = low + at // (2 * count)
            parts = [
                weights[chunk, half, block, spot, place]
                for spot in (place, 1 - place)
                for half in range(2)
            ]
            acc[chunk] += jnp.dot(
                normed[2 * block + place],
                jnp.concatenate(parts, axis=0),
                preferred_element_type=jnp.float32,
            )

    w_start(3)
    w_one(2)
    z_start("away", 1)
    w_four(0)
    z_forward("home", 0)
    z_forward("home", 1)
    w_three(1)
    w_two(2)
    w_start(4)
    w_one(3)
    w_wait(0)
    project((0, 1), 0, 1)
    w_four(1)
    w_three(2)
    w_two(3)
    w_one(4)
    w_wait(1)
    project((1, 1), 0, 1)
    z_forward("away", 0)
    z_forward("away", 1)
    w_four(2)
    w_three(3)
    w_two(4)
    for at in ((0, 1), (1, 0)):
        arrive([z_near[at]])
    project((0, 2), 1, 2)
    w_four(3)
    w_three(4)
    w_wait(2)
    project((2, 1), 0, 1)
    project((2, 1), 1, 2)
    w_wait(3)
    project((3, 1), 0, 1)
    project((3, 1), 1, 2)
    w_four(4)
    arrive(z_far)

    project((0, 1), 2, 1)
    keys[BACK] = jnp.transpose(acc[0, :, :HEAD_DIM]).astype(jnp.bfloat16)
    values[BACK] = acc[0, :, HEAD_DIM:].astype(jnp.bfloat16)
    kv_copies = [
        remote(
            table.at[BACK],
            table.at[BACK - step],
            kv_send.at[at, step - 1],
            kv_recv.at[at, step - 1],
            **holder(rows_at + step),
        )
        for step in range(1, BACK + 1)
        for at, table in enumerate((keys, values))
    ]
    go(kv_copies)
    project((1, 3), 2, 1)
    w_wait(4)
    project((4, 1), 0, 1)
    project((4, 1), 1, 2)
    project((4, 1), 2, 1)
    arrive(kv_copies)

    def attend(chunk, head):
        columns_here = pl.ds(pl.multiple_of(head * HEAD_DIM, HEAD_DIM), HEAD_DIM)
        tile = 256
        tiles = range(ROWS // tile)
        spans = [slice(r * tile, (r + 1) * tile) for r in tiles]
        query = [acc[chunk, spans[r], columns_here].astype(jnp.bfloat16) for r in tiles]
        run_max = [jnp.full((tile, 1), NEG_FLOOR, jnp.float32) for r in tiles]
        sums = [jnp.zeros((tile, 128), jnp.float32) for r in tiles]
        output = [jnp.zeros((tile, HEAD_DIM), jnp.float32) for r in tiles]
        for j in range(BACK + 1):
            for r in tiles:
                low = r * tile if j == 0 else 0
                high = (r + 1) * tile if j == BACK else STEP
                scores = jnp.dot(
                    query[r], keys[j, :, low:high], preferred_element_type=jnp.float32
                )
                scores = scores * SCALING + bias[j, spans[r], low:high]
                new_max = jnp.maximum(run_max[r], jnp.max(scores, axis=-1, keepdims=True))
                rescale = jnp.exp2(run_max[r] - new_max)
                probs = jnp.exp2(scores - new_max)
                output[r] = output[r] * rescale + jnp.dot(
                    probs.astype(jnp.bfloat16),
                    values[j, low:high, :],
                    preferred_element_type=jnp.float32,
                )
                partial = probs[:, :128]
                for first in range(128, high - low, 128):
                    partial = partial + probs[:, first : first + 128]
                sums[r] = sums[r] * rescale + partial
                run_max[r] = new_max
        for r in tiles:
            total = jnp.sum(sums[r], axis=-1, keepdims=True)
            attended[spans[r], columns_here] = (output[r] / total).astype(jnp.bfloat16)

    own_rows = pl.ds(pl.multiple_of(rows_at * BLOCK, BLOCK), BLOCK)

    def slot_copy(at, span, index, step):
        target = (rows_at + step) % LAYERS
        return remote(
            slots.at[at, pl.ds(pl.multiple_of(target * BLOCK, BLOCK), BLOCK), span],
            landed.at[at, own_rows, span],
            s_send.at[index, step],
            s_recv.at[index, step],
            layer=target,
            attn=group,
        )

    def slot_send(at, first, width, index):
        span = pl.ds(first, width)
        slots[at, :, span] = jnp.dot(
            pick[...], attended[:, span], preferred_element_type=jnp.float32
        ).astype(jnp.bfloat16)
        for step in range(1, LAYERS):
            slot_copy(at, span, index, step).start()
        own = slot_copy(at, span, index, 0)

        @pl.when(away)
        def _():
            own.start()

        @pl.when(home)
        def _():
            landed[at, own_rows, span] = slots[at, own_rows, span]

    def slot_take(at, first, width, index, column):
        span = pl.ds(first, width)
        for step in range(1, LAYERS):
            slot_copy(at, span, index, step).wait()
        own = slot_copy(at, span, index, 0)

        @pl.when(away)
        def _():
            own.wait()

        out_ref[:, pl.ds(column, width)] = jnp.dot(
            keep[...], landed[at, :, span], preferred_element_type=jnp.float32
        ).astype(jnp.bfloat16)

    @pl.loop(0, CHUNKS - 2)
    def _(at):
        @pl.loop(0, 2)
        def _(head):
            attend(at + 1, head)

        slot_send(at, 0, WIDE, at)

        @pl.when(at > 0)
        def _():
            slot_take(at - 1, 0, WIDE, at - 1, pl.multiple_of((at - 1) * WIDE, WIDE))

    last = CHUNKS - 2
    for head in range(2):
        attend(last + 1, head)
        slot_send(last, head * HEAD_DIM, HEAD_DIM, last + head)
        if head == 0:
            slot_take(last - 1, 0, WIDE, last - 1, (last - 1) * WIDE)
    for head in range(2):
        slot_take(
            last, head * HEAD_DIM, HEAD_DIM, last + head, last * WIDE + head * HEAD_DIM
        )

    for who, copies in sent.items():

        def done(copies=copies):
            for copy in copies:
                copy.wait_send()

        if who == "all":
            done()
        else:
            pl.when(condition[who])(done)


def fused(tokens, gain, weight, docs, plan):
    vmem = pl.BlockSpec(memory_space=pltpu.VMEM)
    dma = pltpu.SemaphoreType.DMA
    bf16, f32 = jnp.bfloat16, jnp.float32
    return pl.pallas_call(
        fused_kernel,
        out_shape=jax.ShapeDtypeStruct((ROWS, GROUP * HEAD_DIM), bf16),
        in_specs=[
            vmem,
            vmem,
            pl.BlockSpec(memory_space=pl.ANY),
            vmem,
            pl.BlockSpec(memory_space=pltpu.SMEM),
        ],
        out_specs=vmem,
        scratch_shapes=[
            pltpu.VMEM((ROWS, COLS), bf16),
            pltpu.VMEM((ATTN, ROWS, COLS), bf16),
            pltpu.VMEM((CHUNKS, 2, RING, 2, 2, HALF, WIDE), bf16),
            pltpu.VMEM((BACK + 1, HEAD_DIM, STEP), bf16),
            pltpu.VMEM((BACK + 1, STEP, HEAD_DIM), bf16),
            pltpu.VMEM((BACK + 1, ROWS, STEP), f32),
            pltpu.VMEM((LAYERS * BLOCK, ROWS), bf16),
            pltpu.VMEM((ROWS, LAYERS * BLOCK), bf16),
            pltpu.VMEM((ROWS, WIDE), bf16),
            pltpu.VMEM((CHUNKS - 1, LAYERS * BLOCK, WIDE), bf16),
            pltpu.VMEM((CHUNKS - 1, LAYERS * BLOCK, WIDE), bf16),
            pltpu.VMEM((CHUNKS, ROWS, WIDE), f32),
            pltpu.VMEM((ATTN, 8, ROWS), f32),
            dma((CHUNKS,)),
            dma((CHUNKS, 2)),
            dma((CHUNKS, 2)),
            dma((CHUNKS, 8)),
            dma((CHUNKS, 8)),
            dma((CHUNKS, 4)),
            dma((CHUNKS, 4)),
            dma((2, 2)),
            dma((2, 2)),
            dma((6,)),
            dma((6,)),
            dma((ATTN - 1,)),
            dma((ATTN - 1,)),
            dma((2, BACK)),
            dma((2, BACK)),
            dma((CHUNKS, LAYERS)),
            dma((CHUNKS, LAYERS)),
        ],
        compiler_params=pltpu.CompilerParams(
            collective_id=0, has_side_effects=True, vmem_limit_bytes=60 * 2**20
        ),
        cost_estimate=pl.CostEstimate(
            flops=2 * ROWS * 8192 * 1280, bytes_accessed=30 * 2**20, transcendentals=10 * 2**20
        ),
    )(tokens, gain, weight, docs, plan)


def solution(mesh):
    placed = (P("layer", "attn"), P(), P("layer", "attn"), P(), P())
    return jax.shard_map(
        fused, mesh=mesh, in_specs=placed, out_specs=P("layer", "attn"), check_vma=False
    )
```

time: 621 us -> 159 us (0.26)
  the two profiles are of different devices: /device:TPU:2 before, /device:TPU:1 now
where the time goes in v1:
time: 159 us; the launch traced here: 158 us
  Pallas kernels  156 us (98%)
  local copies, waits for them, and re-layouts  2.26 us (1%)
    pallas_call x1, Pallas kernels, fused(): pl.pallas_call(fused_kernel, out_shape=jax.ShapeDtypeStruct((ROWS, GROUP...  156 us

profile of v1, /device:TPU:1, one launch (start us, length us, event | category | flops | bytes accessed | tf_op | source)
XLA Modules:
  0.0 158.5 jit_solution(12042388836531085334)
XLA Ops:
  0.0 156.2 %shard_map.55 = bf16[512,1024]{1,0:T(8,128)(2,1)} custom-call(bf16[512,1024]{1,0:T(8,128)(2,1)} %tok_ref.1, f32[8192]{0:T(1024)} %gain_ref.1, bf16[512,1280]{1,0:T(8,128)(2,1)} %w_ref.1, s32[8192]{0:T(1024)} %doc_ref.1, s32[128]{0:T(128)} %plan_ref.1), custom_call_target="tpu_custom_call" | custom-call | flops 10737418240 | bytes 31457280 | tf_op jit(solution)/shard_map/pallas_call | solution.py:605
  156.2 2.3 %copy.7 = bf16[512,1024]{1,0:T(8,128)(2,1)} copy(bf16[512,1024]{1,0:T(8,128)(2,1)} %shard_map.55) | data formatting | bytes 2097152

commit v2 on v1

--- a/solution.py
+++ b/solution.py
@@ -396,12 +396,13 @@
         row = doc_ref[pl.ds(pl.multiple_of(source * STEP, STEP), STEP)]
         return row.reshape(1, STEP).astype(jnp.float32)
 
-    row_doc = jnp.transpose(jnp.broadcast_to(doc_row(rows_at), (128, STEP)))[:, :1]
-    row_at = lax.broadcasted_iota(jnp.int32, (ROWS, STEP), 0)
-    key_at = lax.broadcasted_iota(jnp.int32, (ROWS, STEP), 1)
+    row_doc = doc_row(rows_at)
+    key_at = lax.broadcasted_iota(jnp.int32, (STEP, ROWS), 0)
+    row_at = lax.broadcasted_iota(jnp.int32, (STEP, ROWS), 1)
     for j in range(BACK + 1):
         source = rows_at - BACK + j
         key_doc = doc_row((source + LAYERS) % LAYERS)
+        key_doc = jnp.transpose(jnp.broadcast_to(key_doc, (128, STEP)))[:, :1]
         allowed = jnp.where(source < 0, -1.0, key_doc) == row_doc
         if j == BACK:
             allowed = allowed & (key_at <= row_at)
@@ -409,11 +410,12 @@
 
     def project(chunks, first, count):
         low, many = chunks
+        stride = 2 if count == 2 else 1
 
         @pl.loop(0, 2 * count * many)
         def _(at):
             place = at % 2
-            block = (z + first + 2 * ((at // 2) % count)) % RING
+            block = (z + first + stride * ((at // 2) % count)) % RING
             chunk = low + at // (2 * count)
             parts = [
                 weights[chunk, half, block, spot, place]
@@ -452,20 +454,16 @@
     for at in ((0, 1), (1, 0)):
         arrive([z_near[at]])
     project((0, 2), 1, 2)
-    w_four(3)
-    w_three(4)
     w_wait(2)
     project((2, 1), 0, 1)
     project((2, 1), 1, 2)
-    w_wait(3)
-    project((3, 1), 0, 1)
-    project((3, 1), 1, 2)
-    w_four(4)
+    w_four(3)
+    w_three(4)
     arrive(z_far)
 
     project((0, 1), 2, 1)
-    keys[BACK] = jnp.transpose(acc[0, :, :HEAD_DIM]).astype(jnp.bfloat16)
-    values[BACK] = acc[0, :, HEAD_DIM:].astype(jnp.bfloat16)
+    keys[BACK] = acc[0, :, :HEAD_DIM].astype(jnp.bfloat16)
+    values[BACK] = jnp.transpose(acc[0, :, HEAD_DIM:]).astype(jnp.bfloat16)
     kv_copies = [
         remote(
             table.at[BACK],
@@ -478,11 +476,9 @@
         for at, table in enumerate((keys, values))
     ]
     go(kv_copies)
-    project((1, 3), 2, 1)
-    w_wait(4)
-    project((4, 1), 0, 1)
-    project((4, 1), 1, 2)
-    project((4, 1), 2, 1)
+    project((1, 2), 2, 1)
+    w_wait(3)
+    project((3, 1), 0, 4)
     arrive(kv_copies)
 
     def attend(chunk, head):
@@ -490,34 +486,30 @@
         tile = 256
         tiles = range(ROWS // tile)
         spans = [slice(r * tile, (r + 1) * tile) for r in tiles]
-        query = [acc[chunk, spans[r], columns_here].astype(jnp.bfloat16) for r in tiles]
-        run_max = [jnp.full((tile, 1), NEG_FLOOR, jnp.float32) for r in tiles]
-        sums = [jnp.zeros((tile, 128), jnp.float32) for r in tiles]
-        output = [jnp.zeros((tile, HEAD_DIM), jnp.float32) for r in tiles]
+        queries = jnp.transpose(acc[chunk, :, columns_here]).astype(jnp.bfloat16)
+        run_max = [jnp.full((1, tile), NEG_FLOOR, jnp.float32) for r in tiles]
+        sums = [jnp.zeros((1, tile), jnp.float32) for r in tiles]
+        output = [jnp.zeros((HEAD_DIM, tile), jnp.float32) for r in tiles]
         for j in range(BACK + 1):
             for r in tiles:
                 low = r * tile if j == 0 else 0
                 high = (r + 1) * tile if j == BACK else STEP
                 scores = jnp.dot(
-                    query[r], keys[j, :, low:high], preferred_element_type=jnp.float32
+                    keys[j, low:high, :], queries[:, spans[r]], preferred_element_type=jnp.float32
                 )
-                scores = scores * SCALING + bias[j, spans[r], low:high]
-                new_max = jnp.maximum(run_max[r], jnp.max(scores, axis=-1, keepdims=True))
+                scores = scores * SCALING + bias[j, low:high, spans[r]]
+                new_max = jnp.maximum(run_max[r], jnp.max(scores, axis=0, keepdims=True))
                 rescale = jnp.exp2(run_max[r] - new_max)
                 probs = jnp.exp2(scores - new_max)
                 output[r] = output[r] * rescale + jnp.dot(
+                    values[j, :, low:high],
                     probs.astype(jnp.bfloat16),
-                    values[j, low:high, :],
                     preferred_element_type=jnp.float32,
                 )
-                partial = probs[:, :128]
-                for first in range(128, high - low, 128):
-                    partial = partial + probs[:, first : first + 128]
-                sums[r] = sums[r] * rescale + partial
+                sums[r] = sums[r] * rescale + jnp.sum(probs, axis=0, keepdims=True)
                 run_max[r] = new_max
         for r in tiles:
-            total = jnp.sum(sums[r], axis=-1, keepdims=True)
-            attended[spans[r], columns_here] = (output[r] / total).astype(jnp.bfloat16)
+            attended[columns_here, spans[r]] = (output[r] / sums[r]).astype(jnp.bfloat16)
 
     own_rows = pl.ds(pl.multiple_of(rows_at * BLOCK, BLOCK), BLOCK)
 
@@ -534,8 +526,11 @@
 
     def slot_send(at, first, width, index):
         span = pl.ds(first, width)
-        slots[at, :, span] = jnp.dot(
-            pick[...], attended[:, span], preferred_element_type=jnp.float32
+        slots[at, :, span] = lax.dot_general(
+            pick[...],
+            attended[span, :],
+            (((1,), (1,)), ((), ())),
+            preferred_element_type=jnp.float32,
         ).astype(jnp.bfloat16)
         for step in range(1, LAYERS):
             slot_copy(at, span, index, step).start()
@@ -570,6 +565,12 @@
             attend(at + 1, head)
 
         slot_send(at, 0, WIDE, at)
+
+        @pl.when(at == 0)
+        def _():
+            w_four(4)
+            w_wait(4)
+            project((4, 1), 0, 4)
 
         @pl.when(at > 0)
         def _():
@@ -617,12 +618,12 @@
             pltpu.VMEM((ROWS, COLS), bf16),
             pltpu.VMEM((ATTN, ROWS, COLS), bf16),
             pltpu.VMEM((CHUNKS, 2, RING, 2, 2, HALF, WIDE), bf16),
+            pltpu.VMEM((BACK + 1, STEP, HEAD_DIM), bf16),
             pltpu.VMEM((BACK + 1, HEAD_DIM, STEP), bf16),
-            pltpu.VMEM((BACK + 1, STEP, HEAD_DIM), bf16),
-            pltpu.VMEM((BACK + 1, ROWS, STEP), f32),
+            pltpu.VMEM((BACK + 1, STEP, ROWS), f32),
             pltpu.VMEM((LAYERS * BLOCK, ROWS), bf16),
             pltpu.VMEM((ROWS, LAYERS * BLOCK), bf16),
-            pltpu.VMEM((ROWS, WIDE), bf16),
+            pltpu.VMEM((WIDE, ROWS), bf16),
             pltpu.VMEM((CHUNKS - 1, LAYERS * BLOCK, WIDE), bf16),
             pltpu.VMEM((CHUNKS - 1, LAYERS * BLOCK, WIDE), bf16),
             pltpu.VMEM((CHUNKS, ROWS, WIDE), f32),

time: 159 us -> 162 us (1.019)
  Pallas kernels: 156 us -> 160 us
    pallas_call x1, Pallas kernels: 156 us -> 160 us  [fused(): pl.pallas_call(fused_kernel, out_shape=jax.ShapeDtypeStruct((ROWS, GROUP...]
where the time goes in v2:
time: 162 us
  Pallas kernels  160 us (99%)
  local copies, waits for them, and re-layouts  2.26 us (1%)
    pallas_call x1, Pallas kernels, fused(): pl.pallas_call(fused_kernel, out_shape=jax.ShapeDtypeStruct((ROWS, GROUP...  160 us

profile of v2, /device:TPU:1, one launch (start us, length us, event | category | flops | bytes accessed | tf_op | source)
XLA Modules:
  0.0 161.9 jit_solution(17973609295076474608)
XLA Ops:
  0.0 159.7 %shard_map.55 = bf16[512,1024]{1,0:T(8,128)(2,1)} custom-call(bf16[512,1024]{1,0:T(8,128)(2,1)} %tok_ref.1, f32[8192]{0:T(1024)} %gain_ref.1, bf16[512,1280]{1,0:T(8,128)(2,1)} %w_ref.1, s32[8192]{0:T(1024)} %doc_ref.1, s32[128]{0:T(128)} %plan_ref.1), custom_call_target="tpu_custom_call" | custom-call | flops 10737418240 | bytes 31457280 | tf_op jit(solution)/shard_map/pallas_call | solution.py:606
  159.7 2.3 %copy.7 = bf16[512,1024]{1,0:T(8,128)(2,1)} copy(bf16[512,1024]{1,0:T(8,128)(2,1)} %shard_map.55) | data formatting | bytes 2097152

commit v3 on v2

--- a/solution.py
+++ b/solution.py
@@ -71,6 +71,8 @@
     share_recv,
     t_send,
     t_recv,
+    far_send,
+    far_recv,
     m_send,
     m_recv,
     kv_send,
@@ -346,6 +348,16 @@
         for way in range(2)
     }
     z_far = [z_copy(z_rows(z - shift[way], way), 4 + way, way) for way in range(2)]
+    pair_far = [
+        remote(
+            z_rows(z + 2, way),
+            z_rows(z + 2, way),
+            far_send.at[way],
+            far_recv.at[way],
+            layer=partner,
+        )
+        for way in range(2)
+    ]
     share_pair = {half: [share_wait(0, half), share_wait(1, half)] for half in range(2)}
     share_core = {half: [share_wait(1 - core, half)] for half in range(2)}
 
@@ -353,15 +365,19 @@
         arrive(share_core[half] if who == "home" else share_pair[half], who)
         go([z_near[half, 0], z_near[half, 1]], who)
 
-    def z_forward(who, way):
-        arrive([z_near[way, way]], who)
-        go([z_far[way]], who)
+    def z_forward(way):
+        arrive([z_near[way, way]], "home")
+        go([z_far[way]], "home")
+
+    def z_partner(way):
+        arrive([z_far[way]], "home")
+        go([pair_far[way]], "home")
 
     z_start("home", 0)
     z_start("home", 1)
-    w_start(2)
     w_one(0)
     w_two(0)
+    w_start(2)
     w_one(1)
 
     def one_hot(table, first, second, at):
@@ -376,10 +392,6 @@
     for at in range(blocks // 2):
         first = rows_at * blocks + 2 * at
         one_hot(pick, plan_ref[first], plan_ref[first + 1], at)
-
-    z_start("away", 0)
-    w_three(0)
-    w_two(1)
 
     places = []
     count = 0
@@ -391,6 +403,11 @@
         count = count + present
     for at in range(LAYERS // 2):
         one_hot(keep, places[2 * at], places[2 * at + 1], at)
+
+    z_forward(0)
+    w_three(0)
+    w_two(1)
+    z_start("away", 0)
 
     def doc_row(source):
         row = doc_ref[pl.ds(pl.multiple_of(source * STEP, STEP), STEP)]
@@ -430,10 +447,9 @@
 
     w_start(3)
     w_one(2)
+    w_four(0)
+    z_forward(1)
     z_start("away", 1)
-    w_four(0)
-    z_forward("home", 0)
-    z_forward("home", 1)
     w_three(1)
     w_two(2)
     w_start(4)
@@ -441,25 +457,24 @@
     w_wait(0)
     project((0, 1), 0, 1)
     w_four(1)
+    z_partner(0)
     w_three(2)
     w_two(3)
     w_one(4)
     w_wait(1)
     project((1, 1), 0, 1)
-    z_forward("away", 0)
-    z_forward("away", 1)
+    z_partner(1)
     w_four(2)
     w_three(3)
     w_two(4)
-    for at in ((0, 1), (1, 0)):
-        arrive([z_near[at]])
+    arrive([z_near[0, 0], z_near[1, 1]], "away")
+    arrive([z_near[0, 1], z_near[1, 0]])
     project((0, 2), 1, 2)
     w_wait(2)
     project((2, 1), 0, 1)
     project((2, 1), 1, 2)
     w_four(3)
-    w_three(4)
-    arrive(z_far)
+    arrive(pair_far, "away")
 
     project((0, 1), 2, 1)
     keys[BACK] = acc[0, :, :HEAD_DIM].astype(jnp.bfloat16)
@@ -476,40 +491,56 @@
         for at, table in enumerate((keys, values))
     ]
     go(kv_copies)
+    w_three(4)
     project((1, 2), 2, 1)
     w_wait(3)
     project((3, 1), 0, 4)
     arrive(kv_copies)
 
-    def attend(chunk, head):
-        columns_here = pl.ds(pl.multiple_of(head * HEAD_DIM, HEAD_DIM), HEAD_DIM)
+    def over_keys(combine, table):
+        while table.shape[0] > 8:
+            middle = table.shape[0] // 2
+            table = combine(table[:middle], table[middle:])
+        return table
+
+    def attend(chunk, heads):
         tile = 256
-        tiles = range(ROWS // tile)
-        spans = [slice(r * tile, (r + 1) * tile) for r in tiles]
-        queries = jnp.transpose(acc[chunk, :, columns_here]).astype(jnp.bfloat16)
-        run_max = [jnp.full((1, tile), NEG_FLOOR, jnp.float32) for r in tiles]
-        sums = [jnp.zeros((1, tile), jnp.float32) for r in tiles]
-        output = [jnp.zeros((HEAD_DIM, tile), jnp.float32) for r in tiles]
+        spans = [slice(r * tile, (r + 1) * tile) for r in range(ROWS // tile)]
+        chains = [(head, r) for head in heads for r in range(ROWS // tile)]
+        rows_of = {head: slice(head * HEAD_DIM, (head + 1) * HEAD_DIM) for head in heads}
+        queries = {
+            head: jnp.transpose(acc[chunk, :, rows_of[head]]).astype(jnp.bfloat16)
+            for head in heads
+        }
+        run_max = {at: jnp.full((1, tile), NEG_FLOOR, jnp.float32) for at in chains}
+        sums = {at: jnp.zeros((8, tile), jnp.float32) for at in chains}
+        output = {at: jnp.zeros((HEAD_DIM, tile), jnp.float32) for at in chains}
         for j in range(BACK + 1):
-            for r in tiles:
+            for at in chains:
+                head, r = at
                 low = r * tile if j == 0 else 0
                 high = (r + 1) * tile if j == BACK else STEP
                 scores = jnp.dot(
-                    keys[j, low:high, :], queries[:, spans[r]], preferred_element_type=jnp.float32
+                    keys[j, low:high, :],
+                    queries[head][:, spans[r]],
+                    preferred_element_type=jnp.float32,
                 )
                 scores = scores * SCALING + bias[j, low:high, spans[r]]
-                new_max = jnp.maximum(run_max[r], jnp.max(scores, axis=0, keepdims=True))
-                rescale = jnp.exp2(run_max[r] - new_max)
+                top = jnp.max(over_keys(jnp.maximum, scores), axis=0, keepdims=True)
+                new_max = jnp.maximum(run_max[at], top)
+                rescale = jnp.exp2(run_max[at] - new_max)
                 probs = jnp.exp2(scores - new_max)
-                output[r] = output[r] * rescale + jnp.dot(
+                output[at] = output[at] * rescale + jnp.dot(
                     values[j, :, low:high],
                     probs.astype(jnp.bfloat16),
                     preferred_element_type=jnp.float32,
                 )
-                sums[r] = sums[r] * rescale + jnp.sum(probs, axis=0, keepdims=True)
-                run_max[r] = new_max
-        for r in tiles:
-            attended[columns_here, spans[r]] = (output[r] / sums[r]).astype(jnp.bfloat16)
+                sums[at] = sums[at] * rescale + over_keys(jnp.add, probs)
+                run_max[at] = new_max
+        for at in chains:
+            head, r = at
+            total = jnp.sum(sums[at], axis=0, keepdims=True)
+            attended[rows_of[head], spans[r]] = (output[at] / total).astype(jnp.bfloat16)
 
     own_rows = pl.ds(pl.multiple_of(rows_at * BLOCK, BLOCK), BLOCK)
 
@@ -560,10 +591,7 @@
 
     @pl.loop(0, CHUNKS - 2)
     def _(at):
-        @pl.loop(0, 2)
-        def _(head):
-            attend(at + 1, head)
-
+        attend(at + 1, (0, 1))
         slot_send(at, 0, WIDE, at)
 
         @pl.when(at == 0)
@@ -578,7 +606,7 @@
 
     last = CHUNKS - 2
     for head in range(2):
-        attend(last + 1, head)
+        attend(last + 1, (head,))
         slot_send(last, head * HEAD_DIM, HEAD_DIM, last + head)
         if head == 0:
             slot_take(last - 1, 0, WIDE, last - 1, (last - 1) * WIDE)
@@ -639,6 +667,8 @@
             dma((2, 2)),
             dma((6,)),
             dma((6,)),
+            dma((2,)),
+            dma((2,)),
             dma((ATTN - 1,)),
             dma((ATTN - 1,)),
             dma((2, BACK)),

time: 162 us -> 163 us (level)
  no operation moved by 1% of the time
where the time goes in v3:
time: 163 us
  Pallas kernels  161 us (99%)
  local copies, waits for them, and re-layouts  2.26 us (1%)
    pallas_call x1, Pallas kernels, fused(): pl.pallas_call(fused_kernel, out_shape=jax.ShapeDtypeStruct((ROWS, GROUP...  161 us

profile of v3, /device:TPU:1, one launch (start us, length us, event | category | flops | bytes accessed | tf_op | source)
XLA Modules:
  0.0 163.2 jit_solution(773414603288842545)
XLA Ops:
  0.0 161.0 %shard_map.55 = bf16[512,1024]{1,0:T(8,128)(2,1)} custom-call(bf16[512,1024]{1,0:T(8,128)(2,1)} %tok_ref.1, f32[8192]{0:T(1024)} %gain_ref.1, bf16[512,1280]{1,0:T(8,128)(2,1)} %w_ref.1, s32[8192]{0:T(1024)} %doc_ref.1, s32[128]{0:T(128)} %plan_ref.1), custom_call_target="tpu_custom_call" | custom-call | flops 10737418240 | bytes 31457280 | tf_op jit(solution)/shard_map/pallas_call | solution.py:634
  161.0 2.3 %copy.7 = bf16[512,1024]{1,0:T(8,128)(2,1)} copy(bf16[512,1024]{1,0:T(8,128)(2,1)} %shard_map.55) | data formatting | bytes 2097152

commit v4 on v1

--- a/solution.py
+++ b/solution.py
@@ -285,6 +285,7 @@
 
     w_start(0)
     w_start(1)
+    w_start(2)
 
     tokens = tok_ref[...].astype(jnp.float32)
     own_sum = jnp.sum(tokens * tokens, axis=1, keepdims=True)
@@ -359,7 +360,6 @@
 
     z_start("home", 0)
     z_start("home", 1)
-    w_start(2)
     w_one(0)
     w_two(0)
     w_one(1)

time: 159 us -> 157 us (0.987)
  no operation moved by 1% of the time
where the time goes in v4:
time: 157 us
  Pallas kernels  155 us (99%)
  local copies, waits for them, and re-layouts  2.26 us (1%)
    pallas_call x1, Pallas kernels, fused(): pl.pallas_call(fused_kernel, out_shape=jax.ShapeDtypeStruct((ROWS, GROUP...  155 us

profile of v4, /device:TPU:1, one launch (start us, length us, event | category | flops | bytes accessed | tf_op | source)
XLA Modules:
  0.0 157.3 jit_solution(6079991050098045965)
XLA Ops:
  0.0 155.0 %shard_map.55 = bf16[512,1024]{1,0:T(8,128)(2,1)} custom-call(bf16[512,1024]{1,0:T(8,128)(2,1)} %tok_ref.1, f32[8192]{0:T(1024)} %gain_ref.1, bf16[512,1280]{1,0:T(8,128)(2,1)} %w_ref.1, s32[8192]{0:T(1024)} %doc_ref.1, s32[128]{0:T(128)} %plan_ref.1), custom_call_target="tpu_custom_call" | custom-call | flops 10737418240 | bytes 31457280 | tf_op jit(solution)/shard_map/pallas_call | solution.py:605
  155.0 2.3 %copy.7 = bf16[512,1024]{1,0:T(8,128)(2,1)} copy(bf16[512,1024]{1,0:T(8,128)(2,1)} %shard_map.55) | data formatting | bytes 2097152

commit v5 on v4

--- a/solution.py
+++ b/solution.py
@@ -302,6 +302,7 @@
     ]
     go(m_copies)
     acc[...] = jnp.zeros_like(acc)
+    w_one(0)
     arrive(m_copies)
     total = moments[0]
     for at in range(1, ATTN):
@@ -360,7 +361,6 @@
 
     z_start("home", 0)
     z_start("home", 1)
-    w_one(0)
     w_two(0)
     w_one(1)
 

time: 157 us -> 157 us (level)
  no operation moved by 1% of the time
where the time goes in v5:
time: 157 us; the launch traced here: 156 us
  Pallas kernels  154 us (98%)
  local copies, waits for them, and re-layouts  2.26 us (1%)
    pallas_call x1, Pallas kernels, fused(): pl.pallas_call(fused_kernel, out_shape=jax.ShapeDtypeStruct((ROWS, GROUP...  154 us

profile of v5, /device:TPU:1, one launch (start us, length us, event | category | flops | bytes accessed | tf_op | source)
XLA Modules:
  0.0 156.4 jit_solution(3481346104280271840)
XLA Ops:
  0.0 154.1 %shard_map.55 = bf16[512,1024]{1,0:T(8,128)(2,1)} custom-call(bf16[512,1024]{1,0:T(8,128)(2,1)} %tok_ref.1, f32[8192]{0:T(1024)} %gain_ref.1, bf16[512,1280]{1,0:T(8,128)(2,1)} %w_ref.1, s32[8192]{0:T(1024)} %doc_ref.1, s32[128]{0:T(128)} %plan_ref.1), custom_call_target="tpu_custom_call" | custom-call | flops 10737418240 | bytes 31457280 | tf_op jit(solution)/shard_map/pallas_call | solution.py:605
  154.1 2.3 %copy.7 = bf16[512,1024]{1,0:T(8,128)(2,1)} copy(bf16[512,1024]{1,0:T(8,128)(2,1)} %shard_map.55) | data formatting | bytes 2097152
